TPU v7x, 32 devices: a whole 2x2x4 slice. The times are simulated.
32 devices in a mesh: groups: 2 (over x), dp: 16 (over z, y, core), tensor: 1.
Axes of the slice: x: 2, y: 2, z: 4, core: 2. Of those that a mesh axis runs over, the one named last changes fastest.
Arguments:
- token_rows: bfloat16 [512, 7168], P(('groups', 'dp', 'tensor')), parts along dimension 0, may hold values from -6 to 6
- expert_ids: int32 [512, 2], P(('groups', 'dp', 'tensor')), parts along dimension 0, may hold values from 0 to 3, all different within a row; in each aligned block of 16 rows (0 to 15, 16 to 31, ...) at most 16 rows name the same one
- gate_weights: float32 [512, 2], P(('groups', 'dp', 'tensor')), parts along dimension 0, may hold values from 0.2 to 1
- cap_limit: int32 [8], P('groups'), parts along dimension 0, may hold values from 8 to 16, as said below
- queries: bfloat16 [64, 128, 576], P(('groups', 'dp'), 'tensor'), parts along dimension 0, may hold values from -80 to 80
- latent_cache: bfloat16 [64, 512, 576], P(('groups', 'dp')), parts along dimension 0, may hold values from -6 to 6
- lengths: int32 [64], P(('groups', 'dp')), parts along dimension 0, may hold values from 64 to 512, as said below
- w_gate: bfloat16 [7168, 8192], P(None, ('dp', 'tensor')), may hold values from -0.0625 to 0.0625
- w_up: bfloat16 [7168, 8192], P(None, ('dp', 'tensor')), may hold values from -0.0625 to 0.0625
- w_down: bfloat16 [8192, 7168], P(('dp', 'tensor')), may hold values from -0.125 to 0.125
Outputs:
- moe_out: bfloat16 [512, 7168], P(('groups', 'dp', 'tensor')), parts along dimension 0
- context: bfloat16 [64, 128, 512], P(('groups', 'dp'), 'tensor'), parts along dimension 0
There are 2 independent parts, one for each index of `groups`. A program takes and returns all parts, laid end to end along the dimension named above; an argument that names none is the same for every part. Nothing has to cross between parts.
Inputs may be any that keep to these rules, and one draw needn't show every extreme that they name: `expert_ids`: each row names 2 different experts; at most 16 rows of one device name the same expert, and some device's rows reach that. `cap_limit`: copies beyond it, in row order within one device's rows, are dropped. `lengths`: positions 0 to length - 1 of a request are in use.
All inputs are finite; a program needn't handle non-finite values.
Results may differ from a plain program's by a relative error of at most 0.0057.
Values may be sent and summed in bfloat16 or wider, within the bound.
A program may use at most 128 MiB of HBM per device.

v0:
```python
import jax
import jax.numpy as jnp
from jax import lax
from jax.sharding import PartitionSpec as P

LATENT = 512
SPAN = 4


score_scale = 0.07216878364870323


def expert_mlp(flat_rows, gate_cols, up_cols, down_rows):
    gate_part = jnp.dot(flat_rows, gate_cols, preferred_element_type=jnp.float32)
    up_part = jnp.dot(flat_rows, up_cols, preferred_element_type=jnp.float32)
    activated = (jax.nn.silu(gate_part) * up_part).astype(jnp.bfloat16)
    return jnp.dot(activated, down_rows, preferred_element_type=jnp.float32)


def local(
    token_rows,
    expert_ids,
    gate_weights,
    cap_limit,
    queries,
    latent_cache,
    lengths,
    w_gate,
    w_up,
    w_down,
):
    dp_count = lax.axis_size("dp")
    row_count, width = token_rows.shape
    top_count = expert_ids.shape[1]
    experts = cap_limit.shape[0]
    capacity = min(row_count, 2 * row_count * top_count * SPAN // dp_count)
    flat_ids = expert_ids.reshape(-1)
    onehot = (flat_ids[:, None] == jnp.arange(experts, dtype=jnp.int32)[None, :]).astype(jnp.int32)
    before = jnp.cumsum(onehot, axis=0) - onehot
    slot_rank = jnp.sum(before * onehot, axis=1)
    limit_copy = jnp.sum(onehot * cap_limit[None, :], axis=1)
    kept_copy = slot_rank < limit_copy
    owner_expert = jnp.arange(dp_count, dtype=jnp.int32) // SPAN
    slot_ids = jnp.arange(capacity, dtype=jnp.int32)
    pick_table = (
        (owner_expert[:, None, None] == flat_ids[None, None, :])
        & (slot_ids[None, :, None] == slot_rank[None, None, :])
        & kept_copy[None, None, :]
    )
    pick_table = pick_table.reshape(dp_count * capacity, row_count, top_count)
    send_table = jnp.any(pick_table, axis=2).astype(jnp.bfloat16)
    outgoing = jnp.dot(send_table, token_rows, preferred_element_type=jnp.float32).astype(
        jnp.bfloat16
    )
    outgoing = outgoing.reshape(dp_count, capacity, width)
    received = lax.all_to_all(outgoing, "dp", split_axis=0, concat_axis=0, tiled=True)
    shard_rows = lax.all_gather(received, "tensor", axis=0, tiled=True)
    flat_rows = shard_rows.reshape(-1, width)
    partial_terms = expert_mlp(flat_rows, w_gate, w_up, w_down).reshape(
        shard_rows.shape[0], capacity, width
    )
    owner_sum = lax.psum_scatter(partial_terms, "tensor", scatter_dimension=0, tiled=True).astype(
        jnp.bfloat16
    )
    returned = lax.all_to_all(owner_sum, "dp", split_axis=0, concat_axis=0, tiled=True).reshape(
        dp_count * capacity, width
    )
    combined = jnp.zeros((row_count, width), jnp.float32)
    for which in range(top_count):
        table = pick_table[:, :, which].T.astype(jnp.bfloat16)
        summed = jnp.dot(table, returned, preferred_element_type=jnp.float32)
        combined = combined + gate_weights[:, which : which + 1] * summed
    moe_out = combined.astype(jnp.bfloat16)
    scores = (
        jnp.einsum("rhc,rpc->rhp", queries, latent_cache, preferred_element_type=jnp.float32)
        * score_scale
    )
    positions = jnp.arange(latent_cache.shape[1], dtype=jnp.int32)
    in_use = (positions[None, :] < lengths[:, None])[:, None, :]
    masked = jnp.where(in_use, scores, -1e30)
    highest = jnp.max(masked, axis=2, keepdims=True)
    weights = jnp.where(in_use, jnp.exp(masked - highest), 0.0)
    denominator = jnp.sum(weights, axis=2, keepdims=True)
    mixed_sum = jnp.einsum(
        "rhp,rpc->rhc",
        weights.astype(jnp.bfloat16),
        latent_cache[:, :, :LATENT],
        preferred_element_type=jnp.float32,
    )
    context = (mixed_sum / denominator).astype(jnp.bfloat16)
    return (moe_out, context)


def solution(mesh):
    in_specs = (
        P(("groups", "dp", "tensor"), None),
        P(("groups", "dp", "tensor"), None),
        P(("groups", "dp", "tensor"), None),
        P("groups"),
        P(("groups", "dp"), "tensor", None),
        P(("groups", "dp"), None, None),
        P(("groups", "dp")),
        P(None, ("dp", "tensor")),
        P(None, ("dp", "tensor")),
        P(("dp", "tensor"), None),
    )
    out_specs = (P(("groups", "dp", "tensor"), None), P(("groups", "dp"), "tensor", None))
    return jax.shard_map(local, mesh=mesh, in_specs=in_specs, out_specs=out_specs, check_vma=False)
```

profile of v0, /device:TPU:13, one launch (start us, length us, event | category | flops | bytes accessed | tf_op | source)
XLA Modules:
  0.0 201.4 jit_solution(10927191630754238739)
XLA Ops:
  0.6 0.0 copy-start
  0.7 0.8 copy.16
  1.5 0.1 eq.52
  1.5 0.1 fusion.18
  1.6 0.1 reduce_window_sum.11
  1.7 0.8 select_reduce_fusion
  2.5 0.1 iota_compare_fusion.1
  2.6 0.1 broadcast_and_fusion
  2.7 0.2 and.43
  2.9 0.1 lt.28
  3.0 0.1 fusion.28
  3.2 2.1 %convolution_convert_fusion.1 = bf16[256,7168]{1,0:T(8,128)(2,1)S(1)} fusion(pred[256,16]{0,1:T(8,128)(4,1)S(1)} %get-tuple-element.4, bf16[16,7168]{1,0:T(8,128)(2,1)} %param.10), kind=kOutput, calls=%fused_computation.3 | convolution fusion | flops 60555264 | bytes 3903488 | tf_op jit(solution)/shard_map/dot_general | solution.py:52
  5.3 0.0 copy-start.5
  5.3 87.6 %all_to_all.10 = bf16[16,16,7168]{2,1,0:T(8,128)(2,1)S(1)} all-to-all(bf16[16,16,7168]{2,1,0:T(8,128)(2,1)S(1)} %bitcast.29), channel_id=1, replica_groups=mesh['groups'=2,'dp'=16,'tensor'=1] {'dp'}, dimensions={0} | all-to-all | bytes 7340032 | tf_op jit(solution)/shard_map/all_to_all | solution.py:56
  92.9 0.0 copy-start.1
  92.9 1.8 copy-done.1
  94.7 0.0 copy-done.5
  94.7 2.0 %fusion.30 = f32[256,512]{1,0:T(8,128)S(1)} fusion(bf16[256,7168]{1,0:T(8,128)(2,1)S(1)} %bitcast.31, bf16[7168,512]{1,0:T(8,128)(2,1)S(1)} %copy-done.5), kind=kOutput, calls=%fused_computation.51 | convolution fusion | flops 1879048192 | bytes 11534336 | tf_op jit(solution)/shard_map/dot_general | solution.py:14
  96.8 12.1 %convolution_convert_fusion = bf16[256,7168]{1,0:T(8,128)(2,1)} fusion(bf16[512,7168]{1,0:T(8,128)(2,1)} %param.19, bf16[256,7168]{1,0:T(8,128)(2,1)} %bitcast.32, bf16[7168,512]{1,0:T(8,128)(2,1)} %param.18, f32[256,512]{1,0:T(8,128)S(1)} %fusion.30), kind=kOutput, calls=%fused_computation.2 | convolution fusion | flops 3760717824 | bytes 22544384 | tf_op jit(solution)/shard_map/dot_general | solution.py:17
  108.8 0.0 copy-start.3
  108.8 0.0 copy-start.4
  108.8 0.0 copy-start.2
  108.9 5.4 %all-to-all-start.1 = ((bf16[16,16,7168]{2,1,0:T(8,128)(2,1)}), bf16[16,16,7168]{2,1,0:T(8,128)(2,1)}, u32[]{:S(2)}, u32[]{:S(2)}) async-start(bf16[16,16,7168]{2,1,0:T(8,128)(2,1)} %bitcast.30), calls=%async_computation.1 | async-start | bytes 7340032 | tf_op jit(solution)/shard_map/all_to_all | solution.py:65
  114.2 0.0 copy-done.3
  114.2 0.0 copy-done.4
  114.2 0.1 iota_compare_fusion.2
  114.4 0.0 copy-done
  114.4 0.0 copy-done.2
  114.4 0.4 fusion.5
  114.8 0.2 fusion
  115.1 1.2 fusion.8
  116.3 79.2 %all-to-all-done.1 = bf16[16,16,7168]{2,1,0:T(8,128)(2,1)} async-done(((bf16[16,16,7168]{2,1,0:T(8,128)(2,1)}), bf16[16,16,7168]{2,1,0:T(8,128)(2,1)}, u32[]{:S(2)}, u32[]{:S(2)}) %all-to-all-start.1) | async-done | bytes 3670048 | tf_op jit(solution)/shard_map/all_to_all | solution.py:65
  195.5 2.6 %convolution_multiply_fusion = f32[16,7168]{1,0:T(8,128)S(1)} fusion(bf16[256,7168]{1,0:T(8,128)(2,1)} %bitcast.4, f32[16]{0:T(128)S(1)} %get-tuple-element.9, pred[256,16,1]{0,2,1:T(4,128)(4,1)S(1)} %get-tuple-element.7), kind=kOutput, calls=%fused_computation.4 | convolution fusion | flops 58834944 | bytes 4132928 | tf_op jit(solution)/shard_map/dot_general | solution.py:71
  198.1 3.3 %fusion.3 = bf16[16,7168]{1,0:T(8,128)(2,1)} fusion(f32[16,7168]{1,0:T(8,128)S(1)} %convolution_multiply_fusion, bf16[256,7168]{1,0:T(8,128)(2,1)} %bitcast.4, f32[16]{0:T(128)S(1)} %get-tuple-element.8, pred[256,16,1]{0,2,1:T(4,128)(4,1)S(1)} %get-tuple-element.6), kind=kOutput, calls=%fused_computation.7 | convolution fusion | flops 59064320 | bytes 4362304 | tf_op jit(solution)/shard_map/dot_general | solution.py:71
  (4 shorter events, 0.1 us)
Async XLA Ops:
  0.6 113.7 %copy-start = (bf16[2,128,576]{1,2,0:T(8,128)(2,1)S(1)}, bf16[2,128,576]{1,2,0:T(8,128)(2,1)}, u32[]{:S(2)}) copy-start(bf16[2,128,576]{1,2,0:T(8,128)(2,1)} %param.14) | copy-start | bytes 884740
  5.3 89.5 %copy-start.5 = (bf16[7168,512]{1,0:T(8,128)(2,1)S(1)}, bf16[7168,512]{1,0:T(8,128)(2,1)}, u32[]{:S(2)}) copy-start(bf16[7168,512]{1,0:T(8,128)(2,1)} %param.17) | copy-start | bytes 22020100
  92.9 1.8 copy-start.1
  108.8 5.4 %copy-start.3 = (f32[16,2]{0,1:T(2,128)S(1)}, f32[16,2]{0,1:T(2,128)}, u32[]{:S(2)}) copy-start(f32[16,2]{0,1:T(2,128)} %param.12) | copy-start | bytes 388
  108.8 5.4 %copy-start.4 = (s32[2]{0:T(128)S(1)}, s32[2]{0:T(128)}, u32[]{:S(2)}) copy-start(s32[2]{0:T(128)} %param.16) | copy-start | bytes 28
  108.8 5.5 %copy-start.2 = (bf16[2,512,576]{1,2,0:T(8,128)(2,1)S(1)}, bf16[2,512,576]{1,2,0:T(8,128)(2,1)}, u32[]{:S(2)}) copy-start(bf16[2,512,576]{1,2,0:T(8,128)(2,1)} %param.15) | copy-start | bytes 3538948
  108.9 86.6 %all-to-all-start.1 = ((bf16[16,16,7168]{2,1,0:T(8,128)(2,1)}), bf16[16,16,7168]{2,1,0:T(8,128)(2,1)}, u32[]{:S(2)}, u32[]{:S(2)}) async-start(bf16[16,16,7168]{2,1,0:T(8,128)(2,1)} %bitcast.30), calls=%async_computation.1 | async-start | bytes 7340032 | tf_op jit(solution)/shard_map/all_to_all | solution.py:65
where the time goes:
time: 202 us; the launch traced here: 201 us
  blocking collectives  87.6 us (43%)
  waiting for transfers between devices  79.2 us (39%)
  matrix products  23.8 us (12%)
  starting transfers between devices  5.37 us (3%)
  local copies, waits for them, and re-layouts  3.05 us (2%)
    all_to_all x1, blocking collectives, local(): lax.all_to_all(outgoing, 'dp', split_axis=0, concat_axis=0, tiled=True)  87.6 us
    all_to_all x1, waiting for transfers between devices, local(): lax.all_to_all(owner_sum, 'dp', split_axis=0, concat_axis=0, tiled=True)  79.2 us
    dot_general x1, matrix products, expert_mlp(): return jnp.dot(activated, down_rows, preferred_element_type=jnp.float32)  12.1 us
    dot_general x2, matrix products, local(): summed = jnp.dot(table, returned, preferred_element_type=jnp.float32)  5.96 us
    all_to_all x1, starting transfers between devices, local(): lax.all_to_all(owner_sum, 'dp', split_axis=0, concat_axis=0, tiled=True)  5.37 us
  transfers between devices with their start and end apart: 1, of which 1 were waited for; matrix products, arithmetic and copies ran while one was open for 1% of the time, Pallas kernels for 0%

commit v1 on v0

--- a/solution.py
+++ b/solution.py
@@ -1,10 +1,16 @@
+import functools
 import jax
 import jax.numpy as jnp
 from jax import lax
+from jax.experimental import pallas as pl
+from jax.experimental.pallas import tpu as pltpu
 from jax.sharding import PartitionSpec as P
 
 LATENT = 512
 SPAN = 4
+LANES = 128
+GATHER_PARTS = 3
+RETURN_PARTS = 7
 
 
 score_scale = 0.07216878364870323
@@ -91,6 +97,468 @@
     return (moe_out, context)
 
 
+def fused_kernel(
+    planes,
+    gather_parts,
+    return_parts,
+    cap_ref,
+    lengths_ref,
+    rows_ref,
+    ids_ref,
+    gates_ref,
+    queries_hbm,
+    cache_hbm,
+    gate_hbm,
+    up_hbm,
+    down_hbm,
+    moe_ref,
+    context_ref,
+    rows_all,
+    gate_w,
+    up_w,
+    down_w,
+    queries,
+    cache,
+    gate_acc,
+    up_acc,
+    partial,
+    from_core,
+    from_y,
+    plane_sum,
+    from_below,
+    from_above,
+    final,
+    load_sem,
+    attn_sem,
+    in_sem,
+    up_sem,
+    dn_sem,
+    y_sem,
+    core_sem,
+    rcore_sem,
+    ry_sem,
+    rup_sem,
+    rdn_sem,
+):
+    last = planes - 1
+    place = lax.axis_index("dp")
+    z, y, core = place // 4, (place // 2) % 2, place % 2
+    dev = lambda zz, yy, cc: {"dp": zz * 4 + yy * 2 + cc}
+    slot = lambda zz, yy, cc: cc * (2 * planes) + yy * planes + zz
+    width = rows_ref.shape[1]
+    block = rows_ref.shape[0]
+    slots = 4 * planes
+    part = rows_all.shape[3]
+    depths = [min(part, width - part * c) for c in range(gather_parts)]
+    out_part = partial.shape[3]
+
+    attn_copies = [
+        pltpu.make_async_copy(queries_hbm, queries, attn_sem.at[0]),
+        pltpu.make_async_copy(cache_hbm, cache, attn_sem.at[1]),
+    ]
+    weight_copies = []
+    for c in range(gather_parts):
+        span = pl.ds(c * part, depths[c])
+        weight_copies.append(pltpu.make_async_copy(gate_hbm.at[span], gate_w.at[span], load_sem.at[c]))
+        weight_copies.append(pltpu.make_async_copy(up_hbm.at[span], up_w.at[span], load_sem.at[gather_parts + c]))
+    down_copy = pltpu.make_async_copy(down_hbm, down_w, load_sem.at[2 * gather_parts])
+    for copy in attn_copies + weight_copies + [down_copy]:
+        copy.start()
+
+    barrier = pltpu.get_barrier_semaphore()
+    pl.semaphore_signal(barrier, inc=1, device_id=dev(z, 1 - y, core), device_id_type=pl.DeviceIdType.MESH)
+    pl.semaphore_signal(barrier, inc=1, device_id=dev(z, y, 1 - core), device_id_type=pl.DeviceIdType.MESH)
+
+    @pl.when(z > 0)
+    def _():
+        pl.semaphore_signal(barrier, inc=1, device_id=dev(z - 1, y, core), device_id_type=pl.DeviceIdType.MESH)
+
+    @pl.when(z < last)
+    def _():
+        pl.semaphore_signal(barrier, inc=1, device_id=dev(z + 1, y, core), device_id_type=pl.DeviceIdType.MESH)
+
+    own = slot(z, y, core)
+    for c in range(gather_parts):
+        rows_all[c, own, :, : depths[c]] = rows_ref[:, c * part : c * part + depths[c]]
+    experts = cap_ref.shape[0]
+    expert = lax.broadcasted_iota(jnp.int32, (8, block), 0)
+    first, second = expert == ids_ref[0:1, :], expert == ids_ref[1:2, :]
+    named = jnp.where(first | second, 1.0, 0.0)
+    earlier = jnp.where(
+        lax.broadcasted_iota(jnp.int32, (block, block), 0) < lax.broadcasted_iota(jnp.int32, (block, block), 1), 1.0, 0.0
+    )
+    rank = jnp.dot(named.astype(jnp.bfloat16), earlier.astype(jnp.bfloat16), preferred_element_type=jnp.float32)
+    limit = jnp.zeros((8, block), jnp.float32)
+    for e in range(experts):
+        limit = jnp.where(expert == e, cap_ref[e].astype(jnp.float32), limit)
+    weight = jnp.where(first, gates_ref[0:1, :], 0.0) + jnp.where(second, gates_ref[1:2, :], 0.0)
+    weight = jnp.where(rank < limit, weight, 0.0)
+    spread = jnp.zeros((block, LANES), jnp.float32)
+    for term in range(3):
+        rounded = weight.astype(jnp.bfloat16)
+        weight = weight - rounded.astype(jnp.float32)
+        to_lane = (
+            lax.broadcasted_iota(jnp.int32, (8, LANES), 1) == lax.broadcasted_iota(jnp.int32, (8, LANES), 0) + 8 * term
+        )
+        spread = spread + lax.dot_general(
+            rounded,
+            jnp.where(to_lane, 1.0, 0.0).astype(jnp.bfloat16),
+            (((0,), (0,)), ((), ())),
+            preferred_element_type=jnp.float32,
+        )
+    rows_all[gather_parts - 1, own, :, depths[-1] : depths[-1] + LANES] = spread.astype(jnp.bfloat16)
+
+    edges = jnp.where(z > 0, 1, 0) + jnp.where(z < last, 1, 0)
+    pl.semaphore_wait(barrier, 2 + edges)
+
+    def gather_copy(c, where, send, target):
+        return pltpu.make_async_remote_copy(
+            src_ref=rows_all.at[c, where],
+            dst_ref=rows_all.at[c, where],
+            send_sem=send,
+            recv_sem=in_sem.at[c, where],
+            device_id=target,
+            device_id_type=pl.DeviceIdType.MESH,
+        )
+
+    def to_up(c, zz):
+        return gather_copy(c, slot(zz, y, core), up_sem.at[c, zz], dev(z + 1, y, core))
+
+    def to_dn(c, zz):
+        return gather_copy(c, slot(zz, y, core), dn_sem.at[c, zz], dev(z - 1, y, core))
+
+    def to_y(c, zz):
+        return gather_copy(c, slot(zz, y, core), y_sem.at[c, zz], dev(z, 1 - y, core))
+
+    def to_core(c, zz, yy):
+        return gather_copy(c, slot(zz, yy, core), core_sem.at[c, yy * planes + zz], dev(z, y, 1 - core))
+
+    def arrived(c, where):
+        gather_copy(c, where, y_sem.at[c, 0], dev(z, 1 - y, core)).wait_recv()
+
+    @pl.loop(0, gather_parts)
+    def _(c):
+        to_y(c, z).start()
+
+        @pl.when(z < last)
+        def _():
+            to_up(c, z).start()
+
+        @pl.when(z > 0)
+        def _():
+            to_dn(c, z).start()
+
+        to_core(c, z, y).start()
+
+    for copy in attn_copies:
+        copy.wait()
+    for r in range(queries.shape[0]):
+        scores = (
+            lax.dot_general(queries[r], cache[r], (((0,), (0,)), ((), ())), preferred_element_type=jnp.float32)
+            * score_scale
+        )
+        in_use = lax.broadcasted_iota(jnp.int32, scores.shape, 1) < lengths_ref[r]
+        masked = jnp.where(in_use, scores, -1e30)
+        highest = jnp.max(masked, axis=1, keepdims=True)
+        weights = jnp.where(in_use, jnp.exp(masked - highest), 0.0)
+        denominator = jnp.sum(weights, axis=1, keepdims=True)
+        mixed = lax.dot_general(
+            weights.astype(jnp.bfloat16),
+            cache[r, :LATENT, :],
+            (((1,), (1,)), ((), ())),
+            preferred_element_type=jnp.float32,
+        )
+        context_ref[r] = (mixed / denominator).astype(context_ref.dtype)
+
+    def pass_y(c, zz):
+        arrived(c, slot(zz, 1 - y, core))
+        to_core(c, zz, 1 - y).start()
+
+    def pass_y_at(c, d):
+        if d == 0:
+            pass_y(c, z)
+            return
+
+        @pl.when(z >= d)
+        def _():
+            pass_y(c, z - d)
+
+        @pl.when(z + d <= last)
+        def _():
+            pass_y(c, z + d)
+
+    for d in range(1, planes):
+
+        @pl.loop(0, gather_parts)
+        def _(c, d=d):
+            @pl.when(z >= d)
+            def _():
+                arrived(c, slot(z - d, y, core))
+
+                @pl.when(z < last)
+                def _():
+                    to_up(c, z - d).start()
+
+                to_y(c, z - d).start()
+                to_core(c, z - d, y).start()
+
+            @pl.when(z + d <= last)
+            def _():
+                arrived(c, slot(z + d, y, core))
+
+                @pl.when(z > 0)
+                def _():
+                    to_dn(c, z + d).start()
+
+                to_y(c, z + d).start()
+                to_core(c, z + d, y).start()
+
+            pass_y_at(c, d - 1)
+
+    for c in range(gather_parts):
+        pass_y_at(c, last)
+        for yy in range(2):
+            for zz in range(planes):
+                arrived(c, slot(zz, yy, 1 - core))
+        weight_copies[2 * c].wait()
+        weight_copies[2 * c + 1].wait()
+        span = pl.ds(c * part, depths[c])
+        rows = rows_all[c, :, :, : depths[c]].reshape(slots * block, depths[c])
+        gate_part = jnp.dot(rows, gate_w[span], preferred_element_type=jnp.float32)
+        up_part = jnp.dot(rows, up_w[span], preferred_element_type=jnp.float32)
+        if c > 0:
+            gate_part, up_part = gate_part + gate_acc[...], up_part + up_acc[...]
+        if c < gather_parts - 1:
+            gate_acc[...] = gate_part
+            up_acc[...] = up_part
+    activated = ((gate_part / (1.0 + jnp.exp(-gate_part))) * up_part).astype(jnp.bfloat16)
+    terms = rows_all[gather_parts - 1, :, :, depths[-1] : depths[-1] + LANES].reshape(slots * block, LANES)
+    lane = lax.broadcasted_iota(jnp.int32, (slots * block, LANES), 1)
+    factor = jnp.sum(
+        jnp.where((lane == z) | (lane == z + 8) | (lane == z + 16), terms.astype(jnp.float32), 0.0), axis=1, keepdims=True
+    )
+    down_copy.wait()
+
+    half = 2 * planes
+
+    def core_copy(c):
+        return pltpu.make_async_remote_copy(
+            src_ref=partial.at[c, pl.ds((1 - core) * half, half)],
+            dst_ref=from_core.at[c],
+            send_sem=rcore_sem.at[0, c],
+            recv_sem=rcore_sem.at[1, c],
+            device_id=dev(z, y, 1 - core),
+            device_id_type=pl.DeviceIdType.MESH,
+        )
+
+    def y_copy(c):
+        return pltpu.make_async_remote_copy(
+            src_ref=from_core.at[c, pl.ds((1 - y) * planes, planes)],
+            dst_ref=from_y.at[c],
+            send_sem=ry_sem.at[0, c],
+            recv_sem=ry_sem.at[1, c],
+            device_id=dev(z, 1 - y, core),
+            device_id_type=pl.DeviceIdType.MESH,
+        )
+
+    def z_copy(src, dst, sem, c, k, target):
+        return pltpu.make_async_remote_copy(
+            src_ref=src.at[c, k],
+            dst_ref=dst.at[c, k],
+            send_sem=sem.at[0, c, k],
+            recv_sem=sem.at[1, c, k],
+            device_id=target,
+            device_id_type=pl.DeviceIdType.MESH,
+        )
+
+    def up_copy(c, k, src):
+        return z_copy(src, from_below, rup_sem, c, k, dev(z + 1, y, core))
+
+    def dn_copy(c, k, src):
+        return z_copy(src, from_above, rdn_sem, c, k, dev(z - 1, y, core))
+
+    f32 = lambda value: value.astype(jnp.float32)
+
+    def join_core(c):
+        core_copy(c).wait_recv()
+        far = pl.ds((1 - y) * planes, planes)
+        mine = partial[c, pl.ds(core * half + (1 - y) * planes, planes)]
+        from_core[c, far] = (f32(mine) + f32(from_core[c, far])).astype(jnp.bfloat16)
+        y_copy(c).start()
+
+    for c in range(return_parts):
+        result = jnp.dot(
+            activated, down_w[:, c * out_part : (c + 1) * out_part], preferred_element_type=jnp.float32
+        )
+        partial[c] = (result * factor).astype(jnp.bfloat16).reshape(slots, block, out_part)
+        core_copy(c).start()
+        if c > 0:
+            join_core(c - 1)
+    join_core(return_parts - 1)
+
+    def hop(c, k, held, sem, copy):
+        z_copy(plane_sum, held, sem, c, k, dev(z, 1 - y, core)).wait_recv()
+        held[c, k] = (f32(held[c, k]) + f32(plane_sum[c, k])).astype(jnp.bfloat16)
+        copy(c, k, held).start()
+
+    @pl.loop(0, return_parts + last)
+    def _(t):
+        c_up = t - z
+
+        @pl.when((z > 0) & (c_up >= 0) & (c_up < return_parts))
+        def _():
+            for k in range(last, 0, -1):
+
+                @pl.when(z < k)
+                def _():
+                    hop(c_up, k, from_below, rup_sem, up_copy)
+
+        c_dn = t - (last - z)
+
+        @pl.when((z < last) & (c_dn >= 0) & (c_dn < return_parts))
+        def _():
+            for k in range(last):
+
+                @pl.when(z > k)
+                def _():
+                    hop(c_dn, k, from_above, rdn_sem, dn_copy)
+
+        @pl.when(t < return_parts)
+        def _():
+            y_copy(t).wait_recv()
+            near = pl.ds(y * planes, planes)
+            mine = partial[t, pl.ds(core * half + y * planes, planes)]
+            plane_sum[t] = (f32(mine) + f32(from_core[t, near]) + f32(from_y[t])).astype(jnp.bfloat16)
+
+            @pl.when(z == 0)
+            def _():
+                for k in range(last, 0, -1):
+                    up_copy(t, k, plane_sum).start()
+
+            @pl.when(z == last)
+            def _():
+                for k in range(last):
+                    dn_copy(t, k, plane_sum).start()
+
+    for c in range(return_parts):
+        final[...] = f32(plane_sum[c, z])
+
+        @pl.when(z > 0)
+        def _():
+            up_copy(c, z, plane_sum).wait_recv()
+            final[...] += f32(from_below[c, z])
+
+        @pl.when(z < last)
+        def _():
+            dn_copy(c, z, plane_sum).wait_recv()
+            final[...] += f32(from_above[c, z])
+
+        moe_ref[:, c * out_part : (c + 1) * out_part] = final[...].astype(moe_ref.dtype)
+
+    @pl.loop(0, gather_parts)
+    def _(c):
+        for zz in range(planes):
+            to_y(c, zz).wait_send()
+            to_core(c, zz, 0).wait_send()
+            to_core(c, zz, 1).wait_send()
+
+            @pl.when((z >= zz) & (z < last))
+            def _():
+                to_up(c, zz).wait_send()
+
+            @pl.when((z <= zz) & (z > 0))
+            def _():
+                to_dn(c, zz).wait_send()
+
+    @pl.loop(0, return_parts)
+    def _(c):
+        core_copy(c).wait_send()
+        y_copy(c).wait_send()
+        for k in range(planes):
+
+            @pl.when(z < k)
+            def _():
+                up_copy(c, k, plane_sum).wait_send()
+
+            @pl.when(z > k)
+            def _():
+                dn_copy(c, k, plane_sum).wait_send()
+
+
+def local_fused(
+    token_rows,
+    expert_ids,
+    gate_weights,
+    cap_limit,
+    queries,
+    latent_cache,
+    lengths,
+    w_gate,
+    w_up,
+    w_down,
+):
+    dp_count = lax.axis_size("dp")
+    planes = dp_count // SPAN
+    row_count, width = token_rows.shape
+    hidden = w_gate.shape[1]
+    requests, heads = queries.shape[:2]
+    total = row_count * dp_count
+    gather_parts, return_parts = GATHER_PARTS, RETURN_PARTS
+    part = -(-(width + LANES) // (gather_parts * LANES)) * LANES
+    out_part = width // return_parts
+    bf16, f32 = jnp.bfloat16, jnp.float32
+    any_space = pl.BlockSpec(memory_space=pl.ANY)
+    vmem = pl.BlockSpec(memory_space=pltpu.VMEM)
+    smem = pl.BlockSpec(memory_space=pltpu.SMEM)
+    dma = pltpu.SemaphoreType.DMA
+    queries_t = jnp.swapaxes(queries, 1, 2)
+    cache_t = jnp.swapaxes(latent_cache, 1, 2)
+    back = lambda count: pltpu.VMEM((return_parts, count, row_count, out_part), bf16)
+    return pl.pallas_call(
+        functools.partial(fused_kernel, planes, gather_parts, return_parts),
+        out_shape=(
+            jax.ShapeDtypeStruct((row_count, width), bf16),
+            jax.ShapeDtypeStruct((requests, heads, LATENT), bf16),
+        ),
+        in_specs=[smem, smem, vmem, vmem, vmem] + [any_space] * 5,
+        out_specs=(vmem, vmem),
+        scratch_shapes=[
+            pltpu.VMEM((gather_parts, dp_count, row_count, part), bf16),
+            pltpu.VMEM(w_gate.shape, bf16),
+            pltpu.VMEM(w_up.shape, bf16),
+            pltpu.VMEM(w_down.shape, bf16),
+            pltpu.VMEM(queries_t.shape, bf16),
+            pltpu.VMEM(cache_t.shape, bf16),
+            pltpu.VMEM((total, hidden), f32),
+            pltpu.VMEM((total, hidden), f32),
+            back(dp_count),
+            back(2 * planes),
+            back(planes),
+            back(planes),
+            back(planes),
+            back(planes),
+            pltpu.VMEM((row_count, out_part), f32),
+            dma((2 * gather_parts + 1,)),
+            dma((2,)),
+            dma((gather_parts, dp_count)),
+            dma((gather_parts, planes)),
+            dma((gather_parts, planes)),
+            dma((gather_parts, planes)),
+            dma((gather_parts, 2 * planes)),
+            dma((2, return_parts)),
+            dma((2, return_parts)),
+            dma((2, return_parts, planes)),
+            dma((2, return_parts, planes)),
+        ],
+        compiler_params=pltpu.CompilerParams(
+            collective_id=0, has_side_effects=True, vmem_limit_bytes=58 * 1024 * 1024
+        ),
+        cost_estimate=pl.CostEstimate(
+            flops=6 * total * width * hidden, bytes_accessed=6 * width * hidden, transcendentals=total * hidden
+        ),
+    )(cap_limit, lengths, token_rows, expert_ids.T, gate_weights.T, queries_t, cache_t, w_gate, w_up, w_down)
+
+
 def solution(mesh):
     in_specs = (
         P(("groups", "dp", "tensor"), None),
@@ -105,4 +573,7 @@
         P(("dp", "tensor"), None),
     )
     out_specs = (P(("groups", "dp", "tensor"), None), P(("groups", "dp"), "tensor", None))
-    return jax.shard_map(local, mesh=mesh, in_specs=in_specs, out_specs=out_specs, check_vma=False)
+    planes = mesh.shape["dp"] // SPAN
+    fits = mesh.shape["tensor"] == 1 and mesh.shape["dp"] % SPAN == 0 and 2 <= planes <= 4
+    body = local_fused if fits else local
+    return jax.shard_map(body, mesh=mesh, in_specs=in_specs, out_specs=out_specs, check_vma=False)

time: 202 us -> 71.6 us (0.35)
  the two profiles are of different devices: /device:TPU:13 before, /device:TPU:0 now
where the time goes in v1:
time: 71.6 us; the launch traced here: 71.4 us
  Pallas kernels  67.4 us (94%)
  local copies, waits for them, and re-layouts  3.31 us (5%)
    pallas_call x1, Pallas kernels, local_fused(): pl.pallas_call(functools.partial(fused_kernel, planes, gather_parts, retu...  67.4 us
    unnamed x2, local copies, waits for them, and re-layouts  3.31 us

profile of v1, /device:TPU:0, one launch (start us, length us, event | category | flops | bytes accessed | tf_op | source)
XLA Modules:
  0.0 71.4 jit_solution(13720031119584465442)
XLA Ops:
  0.6 67.4 %shard_map.113 = (bf16[16,7168]{1,0:T(8,128)(2,1)}, bf16[2,128,512]{2,1,0:T(8,128)(2,1)}) custom-call(s32[4]{0:T(128)} %cap_ref.1, s32[2]{0:T(128)} %lengths_ref.1, bf16[16,7168]{1,0:T(8,128)(2,1)} %rows_ref.1, s32[2,16]{1,0:T(2,128)} %bitcast.6, f32[2,16]{1,0:T(2,128)} %bitcast.7, bf16[2,576,128]{2,1,0:T(8,128)(2,1)} %bitcast.5, ...), custom_call_target="tpu_custom_call" | custom-call | flops 5637144576 | bytes 22020096 | tf_op jit(solution)/shard_map/pallas_call | solution.py:517
  68.1 1.6 %copy.14 = bf16[16,7168]{1,0:T(8,128)(2,1)} copy(bf16[16,7168]{1,0:T(8,128)(2,1)} %get-tuple-element.4) | data formatting | bytes 458752
  69.7 1.7 %copy.15 = bf16[2,128,512]{2,1,0:T(8,128)(2,1)} copy(bf16[2,128,512]{2,1,0:T(8,128)(2,1)} %get-tuple-element.5) | data formatting | bytes 524288

commit v2 on v1

--- a/solution.py
+++ b/solution.py
@@ -125,9 +125,7 @@
     from_core,
     from_y,
     plane_sum,
-    from_below,
-    from_above,
-    final,
+    from_planes,
     load_sem,
     attn_sem,
     in_sem,
@@ -137,8 +135,7 @@
     core_sem,
     rcore_sem,
     ry_sem,
-    rup_sem,
-    rdn_sem,
+    rz_sem,
 ):
     last = planes - 1
     place = lax.axis_index("dp")
@@ -169,13 +166,10 @@
     pl.semaphore_signal(barrier, inc=1, device_id=dev(z, 1 - y, core), device_id_type=pl.DeviceIdType.MESH)
     pl.semaphore_signal(barrier, inc=1, device_id=dev(z, y, 1 - core), device_id_type=pl.DeviceIdType.MESH)
 
-    @pl.when(z > 0)
-    def _():
-        pl.semaphore_signal(barrier, inc=1, device_id=dev(z - 1, y, core), device_id_type=pl.DeviceIdType.MESH)
-
-    @pl.when(z < last)
-    def _():
-        pl.semaphore_signal(barrier, inc=1, device_id=dev(z + 1, y, core), device_id_type=pl.DeviceIdType.MESH)
+    for d in range(1, planes):
+        pl.semaphore_signal(
+            barrier, inc=1, device_id=dev((z + d) % planes, y, core), device_id_type=pl.DeviceIdType.MESH
+        )
 
     own = slot(z, y, core)
     for c in range(gather_parts):
@@ -208,8 +202,7 @@
         )
     rows_all[gather_parts - 1, own, :, depths[-1] : depths[-1] + LANES] = spread.astype(jnp.bfloat16)
 
-    edges = jnp.where(z > 0, 1, 0) + jnp.where(z < last, 1, 0)
-    pl.semaphore_wait(barrier, 2 + edges)
+    pl.semaphore_wait(barrier, 2 + last)
 
     def gather_copy(c, where, send, target):
         return pltpu.make_async_remote_copy(
@@ -361,21 +354,25 @@
             device_id_type=pl.DeviceIdType.MESH,
         )
 
-    def z_copy(src, dst, sem, c, k, target):
+    def z_copy(c, k):
         return pltpu.make_async_remote_copy(
-            src_ref=src.at[c, k],
-            dst_ref=dst.at[c, k],
-            send_sem=sem.at[0, c, k],
-            recv_sem=sem.at[1, c, k],
-            device_id=target,
+            src_ref=plane_sum.at[c, k],
+            dst_ref=from_planes.at[c, z],
+            send_sem=rz_sem.at[0, c, k],
+            recv_sem=rz_sem.at[1, c, z],
+            device_id=dev(k, y, core),
             device_id_type=pl.DeviceIdType.MESH,
         )
 
-    def up_copy(c, k, src):
-        return z_copy(src, from_below, rup_sem, c, k, dev(z + 1, y, core))
-
-    def dn_copy(c, k, src):
-        return z_copy(src, from_above, rdn_sem, c, k, dev(z - 1, y, core))
+    def z_arrival(c, k):
+        return pltpu.make_async_remote_copy(
+            src_ref=plane_sum.at[c, z],
+            dst_ref=from_planes.at[c, k],
+            send_sem=rz_sem.at[0, c, k],
+            recv_sem=rz_sem.at[1, c, k],
+            device_id=dev(k, y, core),
+            device_id_type=pl.DeviceIdType.MESH,
+        )
 
     f32 = lambda value: value.astype(jnp.float32)
 
@@ -396,64 +393,23 @@
             join_core(c - 1)
     join_core(return_parts - 1)
 
-    def hop(c, k, held, sem, copy):
-        z_copy(plane_sum, held, sem, c, k, dev(z, 1 - y, core)).wait_recv()
-        held[c, k] = (f32(held[c, k]) + f32(plane_sum[c, k])).astype(jnp.bfloat16)
-        copy(c, k, held).start()
-
-    @pl.loop(0, return_parts + last)
-    def _(t):
-        c_up = t - z
-
-        @pl.when((z > 0) & (c_up >= 0) & (c_up < return_parts))
-        def _():
-            for k in range(last, 0, -1):
-
-                @pl.when(z < k)
-                def _():
-                    hop(c_up, k, from_below, rup_sem, up_copy)
-
-        c_dn = t - (last - z)
-
-        @pl.when((z < last) & (c_dn >= 0) & (c_dn < return_parts))
-        def _():
-            for k in range(last):
-
-                @pl.when(z > k)
-                def _():
-                    hop(c_dn, k, from_above, rdn_sem, dn_copy)
-
-        @pl.when(t < return_parts)
-        def _():
-            y_copy(t).wait_recv()
-            near = pl.ds(y * planes, planes)
-            mine = partial[t, pl.ds(core * half + y * planes, planes)]
-            plane_sum[t] = (f32(mine) + f32(from_core[t, near]) + f32(from_y[t])).astype(jnp.bfloat16)
-
-            @pl.when(z == 0)
-            def _():
-                for k in range(last, 0, -1):
-                    up_copy(t, k, plane_sum).start()
-
-            @pl.when(z == last)
-            def _():
-                for k in range(last):
-                    dn_copy(t, k, plane_sum).start()
+    others = [(z + d) % planes for d in range(1, planes)]
+
+    @pl.loop(0, return_parts)
+    def _(c):
+        y_copy(c).wait_recv()
+        near = pl.ds(y * planes, planes)
+        mine = partial[c, pl.ds(core * half + y * planes, planes)]
+        plane_sum[c] = (f32(mine) + f32(from_core[c, near]) + f32(from_y[c])).astype(jnp.bfloat16)
+        for k in others:
+            z_copy(c, k).start()
 
     for c in range(return_parts):
-        final[...] = f32(plane_sum[c, z])
-
-        @pl.when(z > 0)
-        def _():
-            up_copy(c, z, plane_sum).wait_recv()
-            final[...] += f32(from_below[c, z])
-
-        @pl.when(z < last)
-        def _():
-            dn_copy(c, z, plane_sum).wait_recv()
-            final[...] += f32(from_above[c, z])
-
-        moe_ref[:, c * out_part : (c + 1) * out_part] = final[...].astype(moe_ref.dtype)
+        final = f32(plane_sum[c, z])
+        for k in others:
+            z_arrival(c, k).wait_recv()
+            final = final + f32(from_planes[c, k])
+        moe_ref[:, c * out_part : (c + 1) * out_part] = final.astype(moe_ref.dtype)
 
     @pl.loop(0, gather_parts)
     def _(c):
@@ -474,15 +430,19 @@
     def _(c):
         core_copy(c).wait_send()
         y_copy(c).wait_send()
-        for k in range(planes):
-
-            @pl.when(z < k)
-            def _():
-                up_copy(c, k, plane_sum).wait_send()
-
-            @pl.when(z > k)
-            def _():
-                dn_copy(c, k, plane_sum).wait_send()
+        for k in others:
+            z_copy(c, k).wait_send()
+
+
+def place_kernel(moe_in, context_in, moe_out, context_out, sem):
+    copies = [
+        pltpu.make_async_copy(moe_in, moe_out, sem.at[0]),
+        pltpu.make_async_copy(context_in, context_out, sem.at[1]),
+    ]
+    for copy in copies:
+        copy.start()
+    for copy in copies:
+        copy.wait()
 
 
 def local_fused(
@@ -514,7 +474,7 @@
     queries_t = jnp.swapaxes(queries, 1, 2)
     cache_t = jnp.swapaxes(latent_cache, 1, 2)
     back = lambda count: pltpu.VMEM((return_parts, count, row_count, out_part), bf16)
-    return pl.pallas_call(
+    results = pl.pallas_call(
         functools.partial(fused_kernel, planes, gather_parts, return_parts),
         out_shape=(
             jax.ShapeDtypeStruct((row_count, width), bf16),
@@ -536,8 +496,6 @@
             back(planes),
             back(planes),
             back(planes),
-            back(planes),
-            pltpu.VMEM((row_count, out_part), f32),
             dma((2 * gather_parts + 1,)),
             dma((2,)),
             dma((gather_parts, dp_count)),
@@ -548,7 +506,6 @@
             dma((2, return_parts)),
             dma((2, return_parts)),
             dma((2, return_parts, planes)),
-            dma((2, return_parts, planes)),
         ],
         compiler_params=pltpu.CompilerParams(
             collective_id=0, has_side_effects=True, vmem_limit_bytes=58 * 1024 * 1024
@@ -557,6 +514,13 @@
             flops=6 * total * width * hidden, bytes_accessed=6 * width * hidden, transcendentals=total * hidden
         ),
     )(cap_limit, lengths, token_rows, expert_ids.T, gate_weights.T, queries_t, cache_t, w_gate, w_up, w_down)
+    return pl.pallas_call(
+        place_kernel,
+        out_shape=tuple(jax.ShapeDtypeStruct(r.shape, r.dtype) for r in results),
+        in_specs=[vmem, vmem],
+        out_specs=(any_space, any_space),
+        scratch_shapes=[dma((2,))],
+    )(*results)
 
 
 def solution(mesh):

time: 71.6 us -> 65.9 us (0.920)
  local copies, waits for them, and re-layouts: 3.31 us -> 0 us
  Pallas kernels: 67.4 us -> 65.1 us
    pallas_call x1, Pallas kernels: 67.4 us -> 63.2 us  [local_fused(): pl.pallas_call(functools.partial(fused_kernel, planes, gather_parts, retu...]
    unnamed x2 -> x0, local copies, waits for them, and re-layouts: 3.31 us -> none
    pallas_call x0 -> x1, Pallas kernels: none -> 1.87 us  [local_fused(): pl.pallas_call(place_kernel, out_shape=tuple((jax.ShapeDtypeStruct(r.shap...]
where the time goes in v2:
time: 65.9 us; the launch traced here: 65.8 us
  Pallas kernels  65.1 us (99%)
    pallas_call x1, Pallas kernels, local_fused(): pl.pallas_call(functools.partial(fused_kernel, planes, gather_parts, retu...  63.2 us
    pallas_call x1, Pallas kernels, local_fused(): pl.pallas_call(place_kernel, out_shape=tuple((jax.ShapeDtypeStruct(r.shap...  1.87 us

profile of v2, /device:TPU:0, one launch (start us, length us, event | category | flops | bytes accessed | tf_op | source)
XLA Modules:
  0.0 65.8 jit_solution(2977039912025095781)
XLA Ops:
  0.6 63.2 %shard_map.113 = (bf16[16,7168]{1,0:T(8,128)(2,1)}, bf16[2,128,512]{2,1,0:T(8,128)(2,1)}) custom-call(s32[4]{0:T(128)} %cap_ref.1, s32[2]{0:T(128)} %lengths_ref.1, bf16[16,7168]{1,0:T(8,128)(2,1)} %rows_ref.1, s32[2,16]{1,0:T(2,128)} %bitcast.6, f32[2,16]{1,0:T(2,128)} %bitcast.7, bf16[2,576,128]{2,1,0:T(8,128)(2,1)} %bitcast.5, ...), custom_call_target="tpu_custom_call" | custom-call | flops 5637144576 | bytes 22020096 | tf_op jit(solution)/shard_map/pallas_call | solution.py:477
  63.9 1.9 %shard_map.114 = (bf16[16,7168]{1,0:T(8,128)(2,1)}, bf16[2,128,512]{2,1,0:T(8,128)(2,1)}) custom-call(bf16[16,7168]{1,0:T(8,128)(2,1)} %get-tuple-element.4.moe_in, bf16[2,128,512]{2,1,0:T(8,128)(2,1)} %get-tuple-element.5.context_in), custom_call_target="tpu_custom_call" | custom-call | tf_op jit(solution)/shard_map/pallas_call | solution.py:517
